TPU v7x, 32 devices: a whole 2x2x4 slice. The times are simulated.
32 devices in a mesh: dp: 8 (over z, core), tensor: 4 (over y, x).
Axes of the slice: x: 2, y: 2, z: 4, core: 2. Of those that a mesh axis runs over, the one named last changes fastest.
Arguments:
- attention_inputs: bfloat16 [5120, 8192], P('dp', 'tensor'), may hold values from -6 to 6
- mixing_inputs: bfloat16 [5120, 8192], P('dp', 'tensor'), may hold values from -6 to 6
- feedforward_inputs: bfloat16 [5120, 8192], P('dp', 'tensor'), may hold values from -6 to 6
- hidden_inputs: bfloat16 [5120, 28672], P('dp', 'tensor'), may hold values from -6 to 6
- query_grads: bfloat16 [5120, 8192], P('dp', 'tensor'), may hold values from -6 to 6
- keyvalue_grads: bfloat16 [2, 5120, 1024], P(None, 'dp', 'tensor'), may hold values from -6 to 6
- mixing_grads: bfloat16 [5120, 8192], P('dp', 'tensor'), may hold values from -6 to 6
- gateup_grads: bfloat16 [2, 5120, 28672], P(None, 'dp', 'tensor'), may hold values from -6 to 6
- down_grads: bfloat16 [5120, 8192], P('dp', 'tensor'), may hold values from -6 to 6
- input_bases: bfloat16 [3, 64, 8192], P(None, None, 'tensor'), may hold values from -0.0625 to 0.0625
- hidden_basis: bfloat16 [64, 28672], P(None, 'tensor'), may hold values from -0.03125 to 0.03125
- output_bases: bfloat16 [3, 64, 8192], P(None, None, 'tensor'), may hold values from -0.0625 to 0.0625
- keyvalue_bases: bfloat16 [2, 64, 1024], P(None, None, 'tensor'), may hold values from -0.1875 to 0.1875
- gateup_bases: bfloat16 [2, 64, 28672], P(None, None, 'tensor'), may hold values from -0.03125 to 0.03125
- eigenvalues: float32 [7, 64, 64], replicated, may hold values from 0.05 to 5
- example_lengths: int32 [8, 8], P('dp'), may hold values from 1 to 320, 640 in all within a row
- test_gradients: bfloat16 [1024, 28672], P(('dp', 'tensor')), may hold values from -0.0029907227 to 0.0029907227
Outputs:
- scores: float32 [1024, 64], P(('dp', 'tensor'))
Inputs may be any that keep to these rules, and one draw needn't show every extreme that they name: `example_lengths`: each row holds the lengths of the 8 examples that fill the 640 tokens of one index of dp, in order; they sum to 640, and the longest in every row is exactly 320.
All inputs are finite; a program needn't handle non-finite values.
Results may differ from a plain program's by a relative error of at most 0.0029.
Values may be sent and summed in bfloat16 or wider, within the bound.
A program may use at most 128 MiB of HBM per device.

v0:
```python
import jax
import jax.numpy as jnp
from jax import lax
from jax.sharding import PartitionSpec as P

damping = 0.1


def project_rows(basis_rows, features):
    return lax.dot_general(
        basis_rows, features, (((1,), (1,)), ((), ())), preferred_element_type=jnp.float32
    )


def all_projections(
    attention_inputs,
    mixing_inputs,
    feedforward_inputs,
    hidden_inputs,
    query_grads,
    keyvalue_grads,
    mixing_grads,
    gateup_grads,
    down_grads,
    input_bases,
    hidden_basis,
    output_bases,
    keyvalue_bases,
    gateup_bases,
):
    inputs_side = [
        project_rows(input_bases[0], attention_inputs),
        project_rows(input_bases[1], mixing_inputs),
        project_rows(input_bases[2], feedforward_inputs),
        project_rows(hidden_basis, hidden_inputs),
    ]
    outputs_side = [
        project_rows(output_bases[0], query_grads),
        project_rows(keyvalue_bases[0], keyvalue_grads[0]),
        project_rows(keyvalue_bases[1], keyvalue_grads[1]),
        project_rows(output_bases[1], mixing_grads),
        project_rows(gateup_bases[0], gateup_grads[0]),
        project_rows(gateup_bases[1], gateup_grads[1]),
        project_rows(output_bases[2], down_grads),
    ]
    return jnp.stack(inputs_side + outputs_side)


def example_gradients(inputs, outputs, lengths_row):
    columns = inputs.shape[2]
    finish = jnp.cumsum(lengths_row)
    begins = finish - lengths_row
    position = jnp.arange(columns, dtype=jnp.int32)
    member = jnp.logical_and(
        position[None, :] >= begins[:, None], position[None, :] < finish[:, None]
    ).astype(inputs.dtype)
    masked = member[:, None, None, :] * inputs[None]
    sources = (0, 0, 0, 1, 2, 2, 3)
    blocks = []
    for module in range(7):
        blocks.append(
            jnp.einsum(
                "ot,eit->eoi",
                outputs[module],
                masked[:, sources[module]],
                precision=lax.Precision.HIGHEST,
            )
        )
    return jnp.stack(blocks, axis=1)


def shards(
    attention_inputs,
    mixing_inputs,
    feedforward_inputs,
    hidden_inputs,
    query_grads,
    keyvalue_grads,
    mixing_grads,
    gateup_grads,
    down_grads,
    input_bases,
    hidden_basis,
    output_bases,
    keyvalue_bases,
    gateup_bases,
    eigenvalues,
    example_lengths,
    test_gradients,
):
    partial_terms = all_projections(
        attention_inputs,
        mixing_inputs,
        feedforward_inputs,
        hidden_inputs,
        query_grads,
        keyvalue_grads,
        mixing_grads,
        gateup_grads,
        down_grads,
        input_bases,
        hidden_basis,
        output_bases,
        keyvalue_bases,
        gateup_bases,
    )
    example_count = example_lengths.shape[1]
    projected = lax.psum(partial_terms, "tensor")
    gradients = example_gradients(projected[:4], projected[4:], example_lengths[0])
    scaled = gradients / (eigenvalues[None] + damping)
    flattened = scaled.astype(jnp.bfloat16).reshape(example_count, -1)
    return lax.dot_general(
        test_gradients,
        lax.all_gather(flattened, "dp", axis=0, tiled=True),
        (((1,), (1,)), ((), ())),
        preferred_element_type=jnp.float32,
    )


def solution(mesh):
    in_specs = (
        P("dp", "tensor"),
        P("dp", "tensor"),
        P("dp", "tensor"),
        P("dp", "tensor"),
        P("dp", "tensor"),
        P(None, "dp", "tensor"),
        P("dp", "tensor"),
        P(None, "dp", "tensor"),
        P("dp", "tensor"),
        P(None, None, "tensor"),
        P(None, "tensor"),
        P(None, None, "tensor"),
        P(None, None, "tensor"),
        P(None, None, "tensor"),
        P(),
        P("dp", None),
        P(("dp", "tensor"), None),
    )
    out_specs = P(("dp", "tensor"), None)
    return jax.shard_map(shards, mesh=mesh, in_specs=in_specs, out_specs=out_specs, check_vma=False)
```

profile of v0, /device:TPU:0, one launch (start us, length us, event | category | flops | bytes accessed | tf_op | source)
XLA Modules:
  0.0 185.8 jit_solution(14615538979836323742)
XLA Ops:
  6.5 1.7 copy-done
  8.3 2.7 %fusion.26 = f32[11,64,640]{2,1,0:T(8,128)} fusion(bf16[640,2048]{1,0:T(8,128)(2,1)S(1)} %copy-done, bf16[3,64,2048]{2,1,0:T(8,128)(2,1)} %param.26), kind=kOutput, calls=%fused_computation.40 | convolution fusion | flops 167772160 | bytes 3047424 | tf_op jit(solution)/shard_map/dot_general | solution.py:10
  11.0 2.7 %fusion.25 = f32[11,64,640]{2,1,0:T(8,128)} fusion(f32[11,64,640]{2,1,0:T(8,128)} %fusion.26, bf16[640,2048]{1,0:T(8,128)(2,1)S(1)} %copy-done.2, bf16[3,64,2048]{2,1,0:T(8,128)(2,1)} %param.26), kind=kOutput, calls=%fused_computation.38 | convolution fusion | flops 167772160 | bytes 3047424 | tf_op jit(solution)/shard_map/dot_general | solution.py:10
  13.7 2.6 %fusion.24 = f32[11,64,640]{2,1,0:T(8,128)} fusion(f32[11,64,640]{2,1,0:T(8,128)} %fusion.25, bf16[640,2048]{1,0:T(8,128)(2,1)S(1)} %copy-done.3, bf16[3,64,2048]{2,1,0:T(8,128)(2,1)} %param.26), kind=kOutput, calls=%fused_computation.36 | convolution fusion | flops 167772160 | bytes 3047424 | tf_op jit(solution)/shard_map/dot_general | solution.py:10
  16.3 7.3 %fusion.41 = f32[11,64,640]{2,1,0:T(8,128)} fusion(f32[11,64,640]{2,1,0:T(8,128)} %fusion.24, bf16[64,7168]{1,0:T(8,128)(2,1)S(1)} %copy-done.8, bf16[640,7168]{1,0:T(8,128)(2,1)} %param.20), kind=kOutput, calls=%fused_computation.50 | convolution fusion | flops 587202560 | bytes 10256384 | tf_op jit(solution)/shard_map/dot_general | solution.py:10
  23.6 1.6 fusion.23
  25.2 0.9 fusion.28
  26.1 0.9 fusion.27
  27.0 1.6 fusion.22
  28.6 7.2 %fusion.32 = f32[11,64,640]{2,1,0:T(8,128)} fusion(f32[11,64,640]{2,1,0:T(8,128)} %fusion.22, bf16[2,640,7168]{2,1,0:T(8,128)(2,1)} %param.24, bf16[2,64,7168]{2,1,0:T(8,128)(2,1)S(1)} %copy-done.13), kind=kOutput, calls=%fused_computation.46 | convolution fusion | flops 587202560 | bytes 10256384 | tf_op jit(solution)/shard_map/dot_general | solution.py:10
  35.8 7.3 %fusion.38 = f32[11,64,640]{2,1,0:T(8,128)} fusion(f32[11,64,640]{2,1,0:T(8,128)} %fusion.32, bf16[2,640,7168]{2,1,0:T(8,128)(2,1)} %param.24, bf16[2,64,7168]{2,1,0:T(8,128)(2,1)S(1)} %copy-done.13), kind=kOutput, calls=%fused_computation.48 | convolution fusion | flops 587202560 | bytes 10256384 | tf_op jit(solution)/shard_map/dot_general | solution.py:10
  43.1 1.6 fusion.21
  44.7 0.2 all-gather.2.cloned.1.call-start
  45.0 0.1 div.11
  45.1 0.3 copy-done.14
  45.3 0.2 reduce-window.7
  45.6 66.9 %all-reduce.2.cloned.1.call-done = f32[11,64,640]{2,1,0:T(8,128)} async-done(((f32[11,64,640]{2,1,0:T(8,128)}), f32[11,64,640]{2,1,0:T(8,128)}) %all-reduce.2.cloned.1.call-update) | async-done | bytes 1802256 | tf_op jit(solution)/shard_map/psum | solution.py:108
  112.4 1.1 slice.115
  113.6 0.6 broadcast_multiply_fusion
  114.2 0.9 copy-done.7
  115.1 1.9 %fusion.20 = f32[8,7,64,64]{2,3,0,1:T(8,128)} fusion(f32[8,4,64,640]{3,2,0,1:T(8,128)S(1)} %broadcast_multiply_fusion, f32[11,64,640]{2,1,0:T(8,128)S(1)} %copy-done.7), kind=kOutput, calls=%fused_computation.28 | convolution fusion | flops 251658240 | bytes 1736704 | tf_op jit(solution)/shard_map/ot,eit->eoi/dot_general | solution.py:62
  117.0 1.9 %fusion.19 = f32[8,7,64,64]{2,3,0,1:T(8,128)} fusion(f32[8,7,64,64]{2,3,0,1:T(8,128)} %fusion.20, f32[8,4,64,640]{3,2,0,1:T(8,128)S(1)} %broadcast_multiply_fusion, f32[11,64,640]{2,1,0:T(8,128)S(1)} %copy-done.7), kind=kOutput, calls=%fused_computation.26 | convolution fusion | flops 251658240 | bytes 1736704 | tf_op jit(solution)/shard_map/ot,eit->eoi/dot_general | solution.py:62
  118.9 1.9 %fusion.18 = f32[8,7,64,64]{2,3,0,1:T(8,128)} fusion(f32[8,7,64,64]{2,3,0,1:T(8,128)} %fusion.19, f32[8,4,64,640]{3,2,0,1:T(8,128)S(1)} %broadcast_multiply_fusion, f32[11,64,640]{2,1,0:T(8,128)S(1)} %copy-done.7), kind=kOutput, calls=%fused_computation.24 | convolution fusion | flops 251658240 | bytes 1736704 | tf_op jit(solution)/shard_map/ot,eit->eoi/dot_general | solution.py:62
  120.8 1.9 %fusion.15 = f32[8,7,64,64]{2,3,0,1:T(8,128)} fusion(f32[8,7,64,64]{2,3,0,1:T(8,128)} %fusion.18, f32[8,4,64,640]{3,2,0,1:T(8,128)S(1)} %broadcast_multiply_fusion, f32[11,64,640]{2,1,0:T(8,128)S(1)} %copy-done.7), kind=kOutput, calls=%fused_computation.20 | convolution fusion | flops 251658240 | bytes 1736704 | tf_op jit(solution)/shard_map/ot,eit->eoi/dot_general | solution.py:62
  122.8 1.9 %fusion.11 = f32[8,7,64,64]{2,3,0,1:T(8,128)} fusion(f32[8,7,64,64]{2,3,0,1:T(8,128)} %fusion.15, f32[8,4,64,640]{3,2,0,1:T(8,128)S(1)} %broadcast_multiply_fusion, f32[11,64,640]{2,1,0:T(8,128)S(1)} %copy-done.7), kind=kOutput, calls=%fused_computation.16 | convolution fusion | flops 251658240 | bytes 1736704 | tf_op jit(solution)/shard_map/ot,eit->eoi/dot_general | solution.py:62
  124.7 1.9 %fusion.13 = f32[8,7,64,64]{2,3,0,1:T(8,128)} fusion(f32[8,7,64,64]{2,3,0,1:T(8,128)} %fusion.11, f32[8,4,64,640]{3,2,0,1:T(8,128)S(1)} %broadcast_multiply_fusion, f32[11,64,640]{2,1,0:T(8,128)S(1)} %copy-done.7), kind=kOutput, calls=%fused_computation.18 | convolution fusion | flops 251658240 | bytes 1736704 | tf_op jit(solution)/shard_map/ot,eit->eoi/dot_general | solution.py:62
  126.6 1.9 %fusion.17 = f32[8,7,64,64]{2,3,0,1:T(8,128)} fusion(f32[8,7,64,64]{2,3,0,1:T(8,128)} %fusion.13, f32[8,4,64,640]{3,2,0,1:T(8,128)S(1)} %broadcast_multiply_fusion, f32[11,64,640]{2,1,0:T(8,128)S(1)} %copy-done.7), kind=kOutput, calls=%fused_computation.22 | convolution fusion | flops 251658240 | bytes 1736704 | tf_op jit(solution)/shard_map/ot,eit->eoi/dot_general | solution.py:62
  128.5 1.8 copy.18
  130.3 0.6 stack.82
  130.9 0.9 divide_convert_fusion
  131.9 42.7 %all-gather.2.cloned.1.call-done = bf16[64,28672]{1,0:T(8,128)(2,1)} async-done(((bf16[8,28672]{1,0:T(8,128)(2,1)}), bf16[64,28672]{1,0:T(8,128)(2,1)}) %all-gather.2.cloned.1.call-update) | async-done | bytes 3670032 | tf_op jit(solution)/shard_map/all_gather | solution.py:114
  174.6 4.3 %convolution_bitcast_fusion.12 = f32[32,64]{1,0:T(8,128)} fusion(bf16[64,28672]{1,0:T(8,128)(2,1)} %all-gather.2.cloned.1.call-done, bf16[32,28672]{1,0:T(8,128)(2,1)} %param.33), kind=kOutput, calls=%fused_computation.51 | convolution fusion | flops 117440512 | bytes 5513216 | tf_op jit(solution)/shard_map/dot_general | solution.py:112
  (33 shorter events, 0.2 us)
Async XLA Ops:
  6.5 1.7 copy-start
  6.5 105.9 %all-reduce.2.cloned.1.call-start = ((), (), s32[]{:S(2)}) async-start(), calls=%async_computation | async-start | bytes 3604480 | tf_op jit(solution)/shard_map/psum | solution.py:108
  8.3 2.7 %copy-start.2 = (bf16[640,2048]{1,0:T(8,128)(2,1)S(1)}, bf16[640,2048]{1,0:T(8,128)(2,1)}, u32[]{:S(2)}) copy-start(bf16[640,2048]{1,0:T(8,128)(2,1)} %param.18) | copy-start | bytes 7864324
  11.0 2.7 %copy-start.3 = (bf16[640,2048]{1,0:T(8,128)(2,1)S(1)}, bf16[640,2048]{1,0:T(8,128)(2,1)}, u32[]{:S(2)}) copy-start(bf16[640,2048]{1,0:T(8,128)(2,1)} %param.19) | copy-start | bytes 7864324
  13.7 2.6 %copy-start.8 = (bf16[64,7168]{1,0:T(8,128)(2,1)S(1)}, bf16[64,7168]{1,0:T(8,128)(2,1)}, u32[]{:S(2)}) copy-start(bf16[64,7168]{1,0:T(8,128)(2,1)} %param.27) | copy-start | bytes 2752516
  16.3 7.3 %copy-start.4 = (bf16[640,2048]{1,0:T(8,128)(2,1)S(1)}, bf16[640,2048]{1,0:T(8,128)(2,1)}, u32[]{:S(2)}) copy-start(bf16[640,2048]{1,0:T(8,128)(2,1)} %param.21) | copy-start | bytes 7864324
  16.3 7.3 %copy-start.9 = (bf16[3,64,2048]{2,1,0:T(8,128)(2,1)S(1)}, bf16[3,64,2048]{2,1,0:T(8,128)(2,1)}, u32[]{:S(2)}) copy-start(bf16[3,64,2048]{2,1,0:T(8,128)(2,1)} %param.28) | copy-start | bytes 2359300
  16.3 8.9 %copy-start.10 = (bf16[2,640,256]{2,1,0:T(8,128)(2,1)S(1)}, bf16[2,640,256]{2,1,0:T(8,128)(2,1)}, u32[]{:S(2)}) copy-start(bf16[2,640,256]{2,1,0:T(8,128)(2,1)} %param.22) | copy-start | bytes 1966084
  23.6 1.6 copy-start.12
  23.6 3.4 %copy-start.5 = (bf16[640,2048]{1,0:T(8,128)(2,1)S(1)}, bf16[640,2048]{1,0:T(8,128)(2,1)}, u32[]{:S(2)}) copy-start(bf16[640,2048]{1,0:T(8,128)(2,1)} %param.23) | copy-start | bytes 7864324
  26.1 2.5 %copy-start.13 = (bf16[2,64,7168]{2,1,0:T(8,128)(2,1)S(1)}, bf16[2,64,7168]{2,1,0:T(8,128)(2,1)}, u32[]{:S(2)}) copy-start(bf16[2,64,7168]{2,1,0:T(8,128)(2,1)} %param.30) | copy-start | bytes 5505028
  35.8 7.3 %copy-start.6 = (bf16[640,2048]{1,0:T(8,128)(2,1)S(1)}, bf16[640,2048]{1,0:T(8,128)(2,1)}, u32[]{:S(2)}) copy-start(bf16[640,2048]{1,0:T(8,128)(2,1)} %param.25) | copy-start | bytes 7864324
  43.1 1.8 copy-start.11
  44.7 0.7 copy-start.14
  44.7 129.9 %all-gather.2.cloned.1.call-start = ((), (), s32[]{:S(2)}) async-start(), calls=%async_computation.1 | async-start | bytes 4128768 | tf_op jit(solution)/shard_map/all_gather | solution.py:114
  113.6 1.5 copy-start.7
  131.9 47.1 %copy-start.1 = (bf16[640,2048]{1,0:T(8,128)(2,1)S(1)}, bf16[640,2048]{1,0:T(8,128)(2,1)}, u32[]{:S(2)}) copy-start(bf16[640,2048]{1,0:T(8,128)(2,1)} %param.17) | copy-start | bytes 7864324
Sparse Core Ops, SparseCore 0:
  44.8 67.5 all-reduce.1
  132.0 42.5 all-gather.1
where the time goes:
time: 186 us
  waiting for transfers between devices  110 us (59%)
  matrix products  54.1 us (29%)
  between operations  13.5 us (7%)
  local copies, waits for them, and re-layouts  6.54 us (4%)
    psum x1, waiting for transfers between devices, shards(): projected = lax.psum(partial_terms, 'tensor')  66.9 us
    all_gather x1, waiting for transfers between devices, shards(): lax.all_gather(flattened, 'dp', axis=0, tiled=True)  42.7 us
    dot_general x11, matrix products, project_rows(): lax.dot_general(basis_rows, features, (((1,), (1,)), ((), ())), preferred...  36.3 us
    dot_general x7, matrix products, example_gradients(): jnp.einsum('ot,eit->eoi', outputs[module], masked[:, sources[module]], pr...  13.5 us
    dot_general x1, matrix products, shards(): lax.dot_general(test_gradients, lax.all_gather(flattened, 'dp', axis=0, t...  4.3 us
  transfers between devices with their start and end apart: 2, of which 2 were waited for; matrix products, arithmetic and copies ran while one was open for 0% of the time, Pallas kernels for 0%

commit v1 on v0

v1 whole, which is shorter than its diff:
```python
import functools

import jax
import jax.numpy as jnp
from jax import lax
from jax.experimental import pallas as pl
from jax.experimental.pallas import tpu as pltpu
from jax.sharding import PartitionSpec as P

damping = 0.1
MESH = pl.DeviceIdType.MESH
GROUP = 4
CHUNK = 128
SLOTS = 4

SOURCES = (0, 0, 0, 1, 2, 2, 3)
NT = (((1,), (1,)), ((), ()))


def input_pair(index, shares, modules, rank):
    start = index * (modules * rank // shares)
    return min(SOURCES[start // rank], max(SOURCES) - 1)


def body(
    dp, shares, attention, mixing, feedforward, hidden, query, keyvalue, mixing_g, gateup, down,
    input_bases, hidden_basis, output_bases, keyvalue_bases, gateup_bases, eigen, lengths, test,
    scores,
    narrow, wide, kv, bases_in, basis_hidden, bases_out, bases_kv, bases_gu,
    part_in, part_out, got_in, got_out, tests, r_hi, r_lo, grads, scaled_f, scaled, gathered, spread, partial, got_partial,
    load_sem, base_sem, in_send, in_recv, out_send, out_recv, test_send, test_recv, test_local,
    grad_send, grad_recv, grad_local, fin_send, fin_recv,
):
    me_dp, me = lax.axis_index("dp"), lax.axis_index("tensor")
    total = dp * shares
    ident = me_dp * shares + me
    tokens = attention.shape[0]
    rank = input_bases.shape[1]
    modules = len(SOURCES)
    rows = modules * rank // shares
    examples = lengths.shape[1]
    lane = me_dp % GROUP
    group_at = me_dp - lane
    width = tests.shape[2] // shares
    pairs = rows // 2
    piece = pairs // GROUP

    units = [
        ("n", attention, None, bases_in, 0, 0),
        ("n", mixing, None, bases_in, 1, 1),
        ("n", feedforward, None, bases_in, 2, 2),
        ("n", query, None, bases_out, 0, 4),
        ("k", keyvalue, None, bases_kv, None, 5),
        ("n", mixing_g, None, bases_out, 1, 7),
        ("n", down, None, bases_out, 2, 10),
        ("w", hidden, None, basis_hidden, None, 3),
        ("w", gateup, 0, bases_gu, 0, 8),
        ("w", gateup, 1, bases_gu, 1, 9),
    ]
    steps = []
    count = {"n": 0, "w": 0, "k": 0}
    for kind, array, at, basis, basis_at, unit in units:
        for chunk in range(tokens // CHUNK if kind == "w" else 1):
            slot = count[kind] % SLOTS
            count[kind] += 1
            steps.append((kind, array, at, basis, basis_at, unit, chunk, slot))
    last_chunk = tokens // CHUNK - 1

    def load(number):
        kind, array, at, _, _, _, chunk, slot = steps[number]
        if kind == "n":
            return pltpu.make_async_copy(array, narrow.at[slot], load_sem.at[number % SLOTS])
        if kind == "k":
            return pltpu.make_async_copy(array, kv, load_sem.at[number % SLOTS])
        source = array if at is None else array.at[at]
        return pltpu.make_async_copy(
            source.at[pl.ds(chunk * CHUNK, CHUNK)], wide.at[slot], load_sem.at[number % SLOTS]
        )

    base_copies = [
        pltpu.make_async_copy(a, b, base_sem.at[i])
        for i, (a, b) in enumerate(
            [
                (input_bases, bases_in),
                (output_bases, bases_out),
                (keyvalue_bases, bases_kv),
                (hidden_basis, basis_hidden),
                (gateup_bases, bases_gu),
            ]
        )
    ]
    based = {}

    def need_basis(basis):
        for i, ref in enumerate([bases_in, bases_out, bases_kv, basis_hidden, bases_gu]):
            if ref is basis and i not in based:
                base_copies[i].wait()
                based[i] = True

    base_copies[0].start()
    for number in range(SLOTS):
        load(number).start()
    for copy in base_copies[1:]:
        copy.start()

    barrier = pltpu.get_barrier_semaphore()

    def greet(k, carry):
        other = (ident + k) % total
        pl.semaphore_signal(
            barrier, inc=1, device_id=(other // shares, other % shares), device_id_type=MESH
        )
        return carry

    lax.fori_loop(1, total, greet, 0)

    def test_copy(j, t, source_lane):
        return pltpu.make_async_remote_copy(
            src_ref=test.at[:, pl.ds(pl.multiple_of((t * GROUP + j) * width, 128), width)],
            dst_ref=tests.at[source_lane, :, pl.ds(t * width, width)],
            send_sem=test_send.at[j, t],
            recv_sem=test_recv.at[source_lane, t],
            device_id=(group_at + j, me),
            device_id_type=MESH,
        )

    def own_test(t):
        return pltpu.make_async_copy(
            test.at[:, pl.ds(pl.multiple_of((t * GROUP + lane) * width, 128), width)],
            tests.at[lane, :, pl.ds(t * width, width)],
            test_local.at[t],
        )

    def in_copy(unit, target, source):
        slot = unit - input_pair(target, shares, modules, rank)
        return pltpu.make_async_remote_copy(
            src_ref=part_in.at[pl.ds(unit * rank, rank)],
            dst_ref=got_in.at[source, pl.ds(slot * rank, rank)],
            send_sem=in_send.at[unit, target],
            recv_sem=in_recv.at[source, slot],
            device_id=(me_dp, target),
            device_id_type=MESH,
        )

    pieces = []
    for target in range(shares):
        low, high = target * rows, (target + 1) * rows
        number = 0
        for module in range(modules):
            first, end = max(low, module * rank), min(high, (module + 1) * rank)
            if first < end:
                pieces.append((module, first, end - first, target, number))
                number += 1

    def out_copy(index, source):
        module, first, size, target, number = pieces[index]
        return pltpu.make_async_remote_copy(
            src_ref=part_out.at[pl.ds(first, size)],
            dst_ref=got_out.at[source, pl.ds(first - target * rows, size)],
            send_sem=out_send.at[index],
            recv_sem=out_recv.at[source, number],
            device_id=(me_dp, target),
            device_id_type=MESH,
        )

    def in_targets(unit):
        return [
            t for t in range(shares) if 0 <= unit - input_pair(t, shares, modules, rank) <= 1
        ]

    def send_unit(unit):
        if unit < 4:
            for target in in_targets(unit):
                @pl.when(me != target)
                def _():
                    in_copy(unit, target, me).start()
        else:
            for index, entry in enumerate(pieces):
                if entry[0] == unit - 4:
                    @pl.when(me != entry[3])
                    def _():
                        out_copy(index, me).start()

    def store(unit, columns, value):
        if unit < 4:
            part_in[pl.ds(unit * rank, rank), columns] = value.T
        else:
            part_out[pl.ds((unit - 4) * rank, rank), columns] = value.T

    def project(features, basis):
        return lax.dot_general(features, basis, NT, preferred_element_type=jnp.float32)

    for number, (kind, _, _, basis, basis_at, unit, chunk, slot) in enumerate(steps):
        need_basis(basis)
        load(number).wait()
        whole = pl.ds(0, tokens)
        if kind == "n":
            store(unit, whole, project(narrow[slot], basis[basis_at]))
        elif kind == "k":
            store(unit, whole, project(kv[0], basis[0]))
            store(unit + 1, whole, project(kv[1], basis[1]))
        else:
            weights = basis[...] if basis_at is None else basis[basis_at]
            store(unit, pl.ds(chunk * CHUNK, CHUNK), project(wide[slot], weights))
        if number + SLOTS < len(steps):
            load(number + SLOTS).start()
        if number == 0:
            pl.semaphore_wait(barrier, total - 1)
            for j in range(GROUP):
                @pl.when(lane != j)
                def _():
                    for t in range(shares):
                        test_copy(j, t, lane).start()
            for t in range(shares):
                own_test(t).start()
        if kind == "k":
            send_unit(unit)
            send_unit(unit + 1)
        elif kind == "n" or chunk == last_chunk:
            send_unit(unit)

    first_in = 0
    for t in range(1, shares):
        step_up = input_pair(t, shares, modules, rank) - input_pair(t - 1, shares, modules, rank)
        if step_up:
            first_in = first_in + step_up * (me >= t).astype(jnp.int32)
    sum_in = part_in[pl.ds(pl.multiple_of(first_in * rank, 8), 2 * rank), :]
    sum_out = part_out[pl.ds(pl.multiple_of(me * rows, 8), rows), :]
    for target in range(shares):
        @pl.when(me == target)
        def _():
            low = input_pair(target, shares, modules, rank)
            for hop in range(1, shares):
                source = (target + hop) % shares
                for unit in (low, low + 1):
                    in_copy(unit, target, source).wait_recv()
                for index, entry in enumerate(pieces):
                    if entry[3] == target:
                        out_copy(index, source).wait_recv()
    for hop in range(1, shares):
        source = (me + hop) % shares
        sum_in = sum_in + got_in[source]
        sum_out = sum_out + got_out[source]

    in_hi = sum_in.astype(jnp.bfloat16)
    in_lo = (sum_in - in_hi.astype(jnp.float32)).astype(jnp.bfloat16)
    out_hi = sum_out.astype(jnp.bfloat16)
    out_lo = (sum_out - out_hi.astype(jnp.float32)).astype(jnp.bfloat16)
    position = lax.broadcasted_iota(jnp.int32, (2 * rank, tokens), 1)
    begin = jnp.int32(0)
    for e in range(examples):
        finish = begin + lengths[0, e]
        member = jnp.logical_and(position >= begin, position < finish).astype(jnp.float32)
        member = member.astype(jnp.bfloat16)
        begin = finish
        hi, lo = in_hi * member, in_lo * member
        for s in range(2):
            r_hi[s, pl.ds(e * rank, rank), :] = hi[s * rank:(s + 1) * rank]
            r_lo[s, pl.ds(e * rank, rank), :] = lo[s * rank:(s + 1) * rank]

    flat_row = me * rows + lax.broadcasted_iota(jnp.int32, (rows, 2 * rank), 0)
    source_of = jnp.zeros((rows, 2 * rank), jnp.int32)
    for module in range(1, modules):
        jump = SOURCES[module] - SOURCES[module - 1]
        if jump:
            source_of = source_of + jump * (flat_row >= module * rank).astype(jnp.int32)
    is_first = source_of == first_in
    damped = eigen[pl.ds(pl.multiple_of(me * rows, 8), rows), :] + damping
    damped = jnp.concatenate([damped, damped], axis=1)
    left = lax.broadcasted_iota(jnp.int32, (pairs, 2 * rank), 1) < rank
    for block in range(examples // 2):
        both = []
        for s in range(2):
            hi = r_hi[s, pl.ds(block * 2 * rank, 2 * rank), :]
            lo = r_lo[s, pl.ds(block * 2 * rank, 2 * rank), :]
            both.append(
                lax.dot_general(out_hi, hi, NT, preferred_element_type=jnp.float32)
                + (
                    lax.dot_general(out_hi, lo, NT, preferred_element_type=jnp.float32)
                    + lax.dot_general(out_lo, hi, NT, preferred_element_type=jnp.float32)
                )
            )
        grads[block] = jnp.where(is_first, both[0], both[1]) / damped
        even = grads[block, pl.ds(0, pairs, stride=2), :]
        odd = grads[block, pl.ds(1, pairs, stride=2), :]
        scaled_f[:, 2 * block, :] = jnp.where(left, even, pltpu.roll(odd, rank, 1))
        scaled_f[:, 2 * block + 1, :] = jnp.where(left, pltpu.roll(even, rank, 1), odd)
    scaled[...] = scaled_f[...].astype(jnp.bfloat16)

    def grad_copy(k):
        other = (ident + k) % total
        other_dp = other // shares
        return pltpu.make_async_remote_copy(
            src_ref=scaled.at[pl.ds((other_dp % GROUP) * piece, piece)],
            dst_ref=gathered.at[me, me_dp],
            send_sem=grad_send.at[k],
            recv_sem=grad_recv.at[ident],
            device_id=(other_dp, other % shares),
            device_id_type=MESH,
        )

    def grad_arrival(k):
        other = (ident + k) % total
        other_dp = other // shares
        return pltpu.make_async_remote_copy(
            src_ref=scaled.at[pl.ds(0, piece)],
            dst_ref=gathered.at[other % shares, other_dp],
            send_sem=grad_send.at[k],
            recv_sem=grad_recv.at[other],
            device_id=(other_dp, other % shares),
            device_id_type=MESH,
        )

    def start_grad(k, carry):
        grad_copy(k).start()
        return carry

    lax.fori_loop(1, total, start_grad, 0)
    own_grad = pltpu.make_async_copy(
        scaled.at[pl.ds(lane * piece, piece)], gathered.at[me, me_dp], grad_local
    )
    own_grad.start()

    for unit in range(4):
        for target in in_targets(unit):
            @pl.when(me != target)
            def _():
                in_copy(unit, target, me).wait_send()
    for index, entry in enumerate(pieces):
        @pl.when(me != entry[3])
        def _():
            out_copy(index, me).wait_send()
    for j in range(GROUP):
        @pl.when(lane != j)
        def _():
            for t in range(shares):
                test_copy(j, t, lane).wait_send()
                test_copy(j, t, j).wait_recv()
    for t in range(shares):
        own_test(t).wait()
    own_grad.wait()

    def finish_grad(k, carry):
        grad_arrival(k).wait_recv()
        return carry

    lax.fori_loop(1, total, finish_grad, 0)

    for t in range(shares):
        for r in range(piece):
            tile = gathered[t, :, r].astype(jnp.float32).reshape(dp * examples, 2 * rank)
            spread[:, pl.ds((t * piece + r) * 2 * rank, 2 * rank)] = tile.astype(jnp.bfloat16)
    queries = tests[...].reshape(GROUP * tests.shape[1], tests.shape[2])
    part = lax.dot_general(queries, spread[...], NT, preferred_element_type=jnp.float32)
    partial[...] = part.reshape(partial.shape)

    def fin_copy(j, source_lane):
        return pltpu.make_async_remote_copy(
            src_ref=partial.at[j],
            dst_ref=got_partial.at[source_lane],
            send_sem=fin_send.at[j],
            recv_sem=fin_recv.at[source_lane],
            device_id=(group_at + j, me),
            device_id_type=MESH,
        )

    for j in range(GROUP):
        @pl.when(lane != j)
        def _():
            fin_copy(j, lane).start()

    def drain_grad(k, carry):
        grad_copy(k).wait_send()
        return carry

    lax.fori_loop(1, total, drain_grad, 0)
    result = partial[lane]
    for j in range(GROUP):
        @pl.when(lane != j)
        def _():
            fin_copy(j, j).wait_recv()
    for hop in range(1, GROUP):
        result = result + got_partial[(lane + hop) % GROUP]
    scores[...] = result
    for j in range(GROUP):
        @pl.when(lane != j)
        def _():
            fin_copy(j, lane).wait_send()


def shards(dp, shares, *arrays):
    (attention, mixing, feedforward, hidden, query, keyvalue, mixing_g, gateup, down,
     input_bases, hidden_basis, output_bases, keyvalue_bases, gateup_bases,
     eigenvalues, lengths, test) = arrays
    tokens, narrow_width = attention.shape
    wide_width = hidden.shape[1]
    rank = input_bases.shape[1]
    modules = len(SOURCES)
    rows = modules * rank // shares
    examples = lengths.shape[1]
    queries, flat = test.shape
    pairs = rows // 2
    piece = pairs // GROUP
    total = dp * shares
    f32, bf16 = jnp.float32, jnp.bfloat16
    V = pltpu.VMEM
    dma = pltpu.SemaphoreType.DMA
    eigen = eigenvalues.reshape(modules * rank, rank)
    any_spec = pl.BlockSpec(memory_space=pl.ANY)
    vmem_spec = pl.BlockSpec(memory_space=V)
    sizes = [a.size * a.dtype.itemsize for a in arrays]
    return pl.pallas_call(
        functools.partial(body, dp, shares),
        out_shape=jax.ShapeDtypeStruct((queries, dp * examples), f32),
        in_specs=[any_spec] * 14
        + [vmem_spec, pl.BlockSpec(memory_space=pltpu.SMEM), any_spec],
        out_specs=vmem_spec,
        scratch_shapes=[
            V((SLOTS, tokens, narrow_width), bf16),
            V((SLOTS, CHUNK, wide_width), bf16),
            V(keyvalue.shape, bf16),
            V(input_bases.shape, bf16),
            V(hidden_basis.shape, bf16),
            V(output_bases.shape, bf16),
            V(keyvalue_bases.shape, bf16),
            V(gateup_bases.shape, bf16),
            V((4 * rank, tokens), f32),
            V((modules * rank, tokens), f32),
            V((shares, 2 * rank, tokens), f32),
            V((shares, rows, tokens), f32),
            V((GROUP, queries, flat // GROUP), bf16),
            V((2, examples * rank, tokens), bf16),
            V((2, examples * rank, tokens), bf16),
            V((examples // 2, rows, 2 * rank), f32),
            V((pairs, examples, 2 * rank), f32),
            V((pairs, examples, 2 * rank), bf16),
            V((shares, dp, piece, examples, 2 * rank), bf16),
            V((dp * examples, flat // GROUP), bf16),
            V((GROUP, queries, dp * examples), f32),
            V((GROUP, queries, dp * examples), f32),
            dma((SLOTS,)),
            dma((5,)),
            dma((4, shares)),
            dma((shares, 2)),
            dma((4 * shares,)),
            dma((shares, 4)),
            dma((GROUP, shares)),
            dma((GROUP, shares)),
            dma((shares,)),
            dma((total,)),
            dma((total,)),
            dma,
            dma((GROUP,)),
            dma((GROUP,)),
        ],
        compiler_params=pltpu.CompilerParams(
            collective_id=0, has_side_effects=True, vmem_limit_bytes=56 * 1024 * 1024
        ),
        cost_estimate=pl.CostEstimate(
            flops=2 * rank * sum(sizes[:9]) // 2, bytes_accessed=sum(sizes), transcendentals=0
        ),
    )(attention, mixing, feedforward, hidden, query, keyvalue, mixing_g, gateup, down,
      input_bases, hidden_basis, output_bases, keyvalue_bases, gateup_bases,
      eigen, lengths, test)


def solution(mesh):
    in_specs = (
        P("dp", "tensor"),
        P("dp", "tensor"),
        P("dp", "tensor"),
        P("dp", "tensor"),
        P("dp", "tensor"),
        P(None, "dp", "tensor"),
        P("dp", "tensor"),
        P(None, "dp", "tensor"),
        P("dp", "tensor"),
        P(None, None, "tensor"),
        P(None, "tensor"),
        P(None, None, "tensor"),
        P(None, None, "tensor"),
        P(None, None, "tensor"),
        P(),
        P("dp", None),
        P(("dp", "tensor"), None),
    )
    out_specs = P(("dp", "tensor"), None)
    run = functools.partial(shards, mesh.shape["dp"], mesh.shape["tensor"])
    return jax.shard_map(run, mesh=mesh, in_specs=in_specs, out_specs=out_specs, check_vma=False)
```

time: 186 us -> 70.1 us (0.38)
  waiting for transfers between devices: 110 us -> 0 us
  Pallas kernels: 0 us -> 68.5 us
  matrix products: 54.1 us -> 0 us
  between operations: 13.5 us -> 0.01 us
  local copies, waits for them, and re-layouts: 6.54 us -> 1.32 us
    pallas_call x0 -> x1, Pallas kernels: none -> 68.5 us  [shards(): pl.pallas_call(functools.partial(body, dp, shares), out_shape=jax.ShapeDt...]
    psum x1 -> x0, waiting for transfers between devices: 66.9 us -> none  [shards(): projected = lax.psum(partial_terms, 'tensor')]
    dot_general x19 -> x0, matrix products: 54.1 us -> none  [the longest x11 36.3 us: project_rows(): lax.dot_general(basis_rows, features, (((1,), (1,)), ((), ())), preferred...]
    all_gather x1 -> x0, waiting for transfers between devices: 42.7 us -> none  [shards(): lax.all_gather(flattened, 'dp', axis=0, tiled=True)]
    another operation x2 -> x0, local copies, waits for them, and re-layouts: 2.4 us -> none  [example_gradients(): return jnp.stack(blocks, axis=1)]
  transfers between devices with their start and end apart: 2 -> 0, of which waited for: 2 -> 0; matrix products, arithmetic and copies ran while one was open for 0% -> 0% of each run, Pallas kernels for 0% -> 0%
where the time goes in v1:
time: 70.1 us; the launch traced here: 69.9 us
  Pallas kernels  68.5 us (98%)
  local copies, waits for them, and re-layouts  1.32 us (2%)
    pallas_call x1, Pallas kernels, shards(): pl.pallas_call(functools.partial(body, dp, shares), out_shape=jax.ShapeDt...  68.5 us

profile of v1, /device:TPU:0, one launch (start us, length us, event | category | flops | bytes accessed | tf_op | source)
XLA Modules:
  0.0 69.9 jit_solution(2079847145247806679)
XLA Ops:
  0.0 68.5 %shard_map.163 = f32[32,64]{1,0:T(8,128)} custom-call(bf16[640,2048]{1,0:T(8,128)(2,1)} %attention.1, bf16[640,2048]{1,0:T(8,128)(2,1)} %mixing.1, bf16[640,2048]{1,0:T(8,128)(2,1)} %feedforward.1, bf16[640,7168]{1,0:T(8,128)(2,1)} %hidden.1, bf16[640,2048]{1,0:T(8,128)(2,1)} %query.1, bf16[2,640,256]{2,1,0:T(8,128)(2,1)} %keyvalue.1, ...), custom_call_target="tpu_custom_call" | custom-call | flops 2810183680 | bytes 50249760 | tf_op jit(solution)/shard_map/pallas_call | solution.py:412
  68.5 1.3 %copy.19 = f32[32,64]{1,0:T(8,128)} copy(f32[32,64]{1,0:T(8,128)} %shard_map.163) | data formatting | bytes 16384
